TPU v7x, 256 devices: a whole 4x4x8 slice. The times are simulated.
256 devices in a mesh: dp: 16 (over y, x_hi, core), tensor: 16 (over z, x_lo).
Axes of the slice: x: 4 (x_hi: 2, x_lo: 2; x = x_hi * 2 + x_lo), y: 4, z: 8, core: 2. Of those that a mesh axis runs over, the one named last changes fastest.
Arguments:
- hidden_in: bfloat16 [4096, 4096], P('dp'), may hold values from -6 to 6
- attn_gain: float32 [4096], replicated, may hold values from 0.5 to 1.5
- qkv_weight: bfloat16 [3, 4096, 4096], P(None, 'dp', 'tensor'), may hold values from -0.09375 to 0.09375
- mix_weight: bfloat16 [4096, 4096], P('tensor', 'dp'), may hold values from -0.09375 to 0.09375
- out_gain: float32 [4096], replicated, may hold values from 0.5 to 1.5
- depth_in_weight: bfloat16 [4096, 1024], P('tensor'), may hold values from -0.09375 to 0.09375
- text_table: bfloat16 [16000, 1024], P('tensor'), may hold values from -6 to 6
- code_tables: bfloat16 [7, 2048, 1024], P(None, 'tensor'), may hold values from -6 to 6
- depth_gain: float32 [1024], replicated, may hold values from 0.5 to 1.5
- depth_qkv: bfloat16 [3, 1024, 1024], P(None, 'dp'), may hold values from -0.1875 to 0.1875
- depth_mix: bfloat16 [1024, 1024], replicated, may hold values from -0.1875 to 0.1875
- final_gain: float32 [1024], replicated, may hold values from 0.5 to 1.5
- heads_weight: bfloat16 [8, 1024, 2048], P(None, None, 'tensor'), may hold values from -0.59765625 to 0.59765625
- text_ids: int32 [4096], P('dp'), may hold values from 0 to 15999
- codes: int32 [4096, 8], P('dp'), may hold values from 0 to 2047
Outputs:
- token_loss: float32 [4096, 8], P(('dp', 'tensor'))
All inputs are finite; a program needn't handle non-finite values.
Results may differ from a plain program's by a relative error of at most 0.005.
Values may be sent and summed in bfloat16 or wider, within the bound.
A program may use at most 128 MiB of HBM per device.

v0:
```python
import math
import jax
import jax.numpy as jnp
from jax import lax
from jax.sharding import PartitionSpec as P

D = 4096
HEAD_DIM = 128
FRAMES = 256
DD = 1024
DHEADS = 16
DHEAD_DIM = 64
CODEBOOKS = 8
epsilon = 1e-05


def rms_factor(values):
    return lax.rsqrt(jnp.mean(values * values, axis=-1, keepdims=True) + epsilon)


def rotate_halves(tensor, positions):
    half_dim = tensor.shape[-1] // 2
    frequency = jnp.exp(jnp.arange(half_dim, dtype=jnp.float32) * (-math.log(10000.0) / half_dim))
    angles = positions[:, None] * frequency[None, :]
    cosine = jnp.cos(angles)[:, None, :]
    sine_part = jnp.sin(angles)[:, None, :]
    first_half = tensor[..., :half_dim]
    second_half = tensor[..., half_dim:]
    return jnp.concatenate(
        [
            first_half * cosine - second_half * sine_part,
            second_half * cosine + first_half * sine_part,
        ],
        axis=-1,
    )


def temporal_mix(normed, qkv_cols):
    row_count = normed.shape[0]
    col_width = qkv_cols.shape[2]
    seq_count = row_count // FRAMES
    head_count = col_width // HEAD_DIM
    projected = jnp.einsum("rd,idw->irw", normed, qkv_cols, preferred_element_type=jnp.float32)
    projected = projected.reshape(3, seq_count, FRAMES, head_count, HEAD_DIM)
    positions = jnp.arange(FRAMES, dtype=jnp.float32)
    queries = rotate_halves(projected[0], positions).astype(jnp.bfloat16)
    keys_rot = rotate_halves(projected[1], positions).astype(jnp.bfloat16)
    values_all = projected[2].astype(jnp.bfloat16)
    scores = jnp.einsum(
        "sqhd,skhd->shqk", queries, keys_rot, preferred_element_type=jnp.float32
    ) * HEAD_DIM ** (-0.5)
    order = jnp.arange(FRAMES)
    causal = order[:, None] >= order[None, :]
    exp_scores = jnp.where(causal, jnp.exp(jnp.where(causal, scores, 0.0)), 0.0)
    weights = (exp_scores / jnp.sum(exp_scores, axis=-1, keepdims=True)).astype(jnp.bfloat16)
    attended = jnp.einsum(
        "shqk,skhd->sqhd", weights, values_all, preferred_element_type=jnp.float32
    )
    return attended.astype(jnp.bfloat16).reshape(row_count, col_width)


def depth_mixer(projected, mix_weight):
    row_count = projected.shape[1]
    split = projected.reshape(3, row_count, CODEBOOKS, DHEADS, DHEAD_DIM)
    scores = jnp.einsum(
        "rqhd,rkhd->rhqk", split[0], split[1], preferred_element_type=jnp.float32
    ) * DHEAD_DIM ** (-0.5)
    order = jnp.arange(CODEBOOKS)
    causal = order[:, None] >= order[None, :]
    exp_scores = jnp.where(causal, jnp.exp(jnp.where(causal, scores, 0.0)), 0.0)
    weights = (exp_scores / jnp.sum(exp_scores, axis=-1, keepdims=True)).astype(jnp.bfloat16)
    attended = jnp.einsum("rhqk,rkhd->rqhd", weights, split[2], preferred_element_type=jnp.float32)
    attended = attended.astype(jnp.bfloat16).reshape(row_count, CODEBOOKS, DD)
    return jnp.einsum("rcd,de->rce", attended, mix_weight, preferred_element_type=jnp.float32)


def local_embeds(text_table, code_tables, text_ids, codes, rank_tensor):
    text_count = text_table.shape[0]
    text_local = text_ids - rank_tensor * text_count
    text_owned = (text_local >= 0) & (text_local < text_count)
    text_found = jnp.take(text_table, jnp.clip(text_local, 0, text_count - 1), axis=0)
    text_part = jnp.where(text_owned[:, None], text_found.astype(jnp.float32), 0.0)
    code_count = code_tables.shape[1]
    code_local = codes[:, : CODEBOOKS - 1] - rank_tensor * code_count
    code_owned = (code_local >= 0) & (code_local < code_count)
    books = jnp.arange(CODEBOOKS - 1, dtype=jnp.int32)[None, :]
    code_found = code_tables[books, jnp.clip(code_local, 0, code_count - 1)]
    code_part = jnp.where(code_owned[:, :, None], code_found.astype(jnp.float32), 0.0)
    return jnp.concatenate([text_part[:, None, :], code_part], axis=1)


def arrive_embeds(embeds):
    return lax.psum_scatter(
        embeds.astype(jnp.bfloat16), "tensor", scatter_dimension=0, tiled=True
    ).astype(jnp.float32)


def shards(
    hidden_in,
    attn_gain,
    qkv_weight,
    mix_weight,
    out_gain,
    depth_in_weight,
    text_table,
    code_tables,
    depth_gain,
    depth_qkv,
    depth_mix,
    final_gain,
    heads_weight,
    text_ids,
    codes,
):
    rank_tensor = lax.axis_index("tensor")
    group_size = lax.axis_size("tensor")
    local_rows = hidden_in.shape[0]
    own_rows = local_rows // group_size
    own_start = rank_tensor * own_rows
    qkv_full, mix_full, depth_full = (
        lax.all_gather(qkv_weight, "dp", axis=1, tiled=True),
        lax.all_gather(mix_weight, "dp", axis=1, tiled=True),
        lax.all_gather(depth_qkv, "dp", axis=1, tiled=True),
    )
    hidden_f = hidden_in.astype(jnp.float32)
    normed = (hidden_f * rms_factor(hidden_f) * attn_gain).astype(jnp.bfloat16)
    attended = temporal_mix(normed, qkv_full)
    partial_mix = jnp.dot(attended, mix_full, preferred_element_type=jnp.float32)
    embeds = local_embeds(text_table, code_tables, text_ids, codes, rank_tensor)
    embed_rows = arrive_embeds(embeds)
    feat_width = depth_in_weight.shape[0]
    feat_start = rank_tensor * feat_width
    summed_cols = lax.psum_scatter(
        partial_mix.astype(jnp.bfloat16), "tensor", scatter_dimension=1, tiled=True
    ).astype(jnp.float32)
    resid_cols = summed_cols + lax.dynamic_slice_in_dim(hidden_f, feat_start, feat_width, 1)
    square_part = jnp.sum(resid_cols * resid_cols, axis=1)
    gain_cols = lax.dynamic_slice_in_dim(out_gain, feat_start, feat_width, 0)
    scaled_cols = (resid_cols * gain_cols).astype(jnp.bfloat16)
    context_part = jnp.dot(scaled_cols, depth_in_weight, preferred_element_type=jnp.float32)
    context_sum, square_sum = (
        lax.psum_scatter(
            context_part.astype(jnp.bfloat16), "tensor", scatter_dimension=0, tiled=True
        ).astype(jnp.float32),
        lax.psum_scatter(
            square_part.astype(jnp.bfloat16), "tensor", scatter_dimension=0, tiled=True
        ).astype(jnp.float32),
    )
    context = context_sum * lax.rsqrt(square_sum / D + epsilon)[:, None]
    depth_input = context[:, None, :] + embed_rows
    dnormed = (depth_input * rms_factor(depth_input) * depth_gain).astype(jnp.bfloat16)
    projected = jnp.einsum("rcd,ide->irce", dnormed, depth_full, preferred_element_type=jnp.float32)
    depth_out = depth_input + depth_mixer(projected.astype(jnp.bfloat16), depth_mix)
    final = (depth_out * rms_factor(depth_out) * final_gain).astype(jnp.bfloat16)
    final_all = lax.all_gather(final, "tensor", axis=0, tiled=True)
    logits = jnp.einsum("rcd,cdv->rcv", final_all, heads_weight, preferred_element_type=jnp.float32)
    vocab_width = heads_weight.shape[2]
    target_local = codes - rank_tensor * vocab_width
    matches = jnp.arange(vocab_width, dtype=jnp.int32)[None, None, :] == target_local[:, :, None]
    target_part = jnp.sum(jnp.where(matches, logits, 0.0), axis=-1)
    exp_part = jnp.sum(jnp.exp(logits), axis=-1)
    exp_total, target_total = lax.psum((exp_part, target_part), "tensor")
    losses = jnp.log(exp_total) - target_total
    return lax.dynamic_slice_in_dim(losses, own_start, own_rows, 0)


def solution(mesh):
    in_specs = (
        P("dp", None),
        P(),
        P(None, "dp", "tensor"),
        P("tensor", "dp"),
        P(),
        P("tensor", None),
        P("tensor", None),
        P(None, "tensor", None),
        P(),
        P(None, "dp", None),
        P(),
        P(),
        P(None, None, "tensor"),
        P("dp"),
        P("dp", None),
    )
    out_specs = P(("dp", "tensor"), None)
    return jax.shard_map(shards, mesh=mesh, in_specs=in_specs, out_specs=out_specs, check_vma=False)
```

profile of v0, /device:TPU:8, one launch (start us, length us, event | category | flops | bytes accessed | tf_op | source)
XLA Modules:
  0.0 645.9 jit_solution(13716090094720428637)
XLA Ops:
  6.5 2.1 copy.45
  8.7 0.7 all-gather.7.cloned.1.call-update
  9.5 0.6 iota_compare_fusion.1
  10.1 2.1 multiply_reduce_fusion
  12.2 0.5 fusion.59
  12.7 70.5 %all-gather.5.cloned.1.call-done = bf16[3,4096,256]{1,2,0:T(8,128)(2,1)} async-done(((bf16[3,256,256]{1,2,0:T(8,128)(2,1)}), bf16[3,4096,256]{1,2,0:T(8,128)(2,1)}) %all-gather.5.cloned.1.call-update) | async-done | bytes 6291472 | tf_op jit(solution)/shard_map/all_gather | solution.py:121
  83.2 5.3 fusion.24
  88.6 0.6 slice.71
  90.0 1.2 fusion.29
  91.2 1.2 convolution_convert_fusion.3
  92.3 43.5 %all-gather.7.cloned.1.call-done = bf16[256,4096]{1,0:T(8,128)(2,1)} async-done(((bf16[256,256]{1,0:T(8,128)(2,1)}), bf16[256,4096]{1,0:T(8,128)(2,1)}) %all-gather.7.cloned.1.call-update) | async-done | bytes 2097168 | tf_op jit(solution)/shard_map/all_gather | solution.py:122
  135.8 3.6 convolution_convert_fusion
  139.6 4.1 convert_element_type.93
  143.8 0.2 reshape.218
  144.0 35.0 %gather_fusion.1 = bf16[1792,1024]{1,0:T(8,128)(2,1)} fusion(bf16[7,128,1024]{2,1,0:T(8,128)(2,1)} %param.22, s32[1792]{0:T(1024)S(1)} %reshape.218), kind=kCustom, calls=%fused_computation.1 | custom fusion | bytes 7354368 | tf_op jit(solution)/shard_map/gather | solution.py:87
  179.0 6.5 %reshape.225 = bf16[256,7,1024]{2,1,0:T(8,128)(2,1)} reshape(bf16[1792,1024]{1,0:T(8,128)(2,1)} %gather_fusion.1) | data formatting | bytes 7340032 | tf_op jit(solution)/shard_map/convert_element_type | solution.py:88
  185.5 0.2 copy.52
  185.7 0.8 dynamic_slice.10
  186.5 3.4 gather_fusion
  189.9 24.1 %reduce-scatter.4.cloned.1.call-done = bf16[256,256]{1,0:T(8,128)(2,1)} async-done(((bf16[256,4096]{1,0:T(8,128)(2,1)}), bf16[256,256]{1,0:T(8,128)(2,1)}) %reduce-scatter.4.cloned.1.call-update) | async-done | bytes 131088 | tf_op jit(solution)/shard_map/reduce_scatter | solution.py:133
  214.0 2.1 convolution_convert_fusion.2
  216.1 0.2 reduce-scatter.8.cloned.1.call-start
  216.3 2.7 select_convert_fusion
  219.0 3.1 fusion.35
  222.2 3.5 pad_maximum_fusion
  225.7 0.5 all-gather.9.cloned.1.call-update
  226.3 0.6 dynamic-slice
  227.6 1.1 multiply_reduce_fusion.3
  228.7 31.8 %all-reduce = bf16[256]{0:T(256)(128)(2,1)S(1)} all-reduce(bf16[256]{0:T(256)(128)(2,1)S(1)} %multiply_reduce_fusion.3), channel_id=4, replica_groups=mesh['dp'=16,'tensor'=16] {'tensor'}, use_global_device_ids=true, to_apply=%region_5.6.clone | all-reduce | flops 256 | bytes 1024
  260.6 25.2 %reduce-scatter.6.cloned.1.call-done = bf16[16,1024]{1,0:T(8,128)(2,1)} async-done(((bf16[256,1024]{1,0:T(8,128)(2,1)}), bf16[16,1024]{1,0:T(8,128)(2,1)}) %reduce-scatter.6.cloned.1.call-update) | async-done | bytes 32784 | tf_op jit(solution)/shard_map/reduce_scatter | solution.py:142
  285.8 0.8 convert_multiply_fusion
  286.6 100.2 %reduce-scatter.8.cloned.1.call-done = bf16[16,8,1024]{2,1,0:T(8,128)(2,1)} async-done(((bf16[256,8,1024]{2,1,0:T(8,128)(2,1)}), bf16[16,8,1024]{2,1,0:T(8,128)(2,1)}) %reduce-scatter.8.cloned.1.call-update) | async-done | bytes 262160 | tf_op jit(solution)/shard_map/reduce_scatter | solution.py:93
  386.8 1.1 multiply_reduce_fusion.2
  387.9 69.5 %all-gather.9.cloned.1.call-done = bf16[3,1024,1024]{2,1,0:T(8,128)(2,1)} async-done(((bf16[3,64,1024]{2,1,0:T(8,128)(2,1)}), bf16[3,1024,1024]{2,1,0:T(8,128)(2,1)}) %all-gather.9.cloned.1.call-update) | async-done | bytes 6291472 | tf_op jit(solution)/shard_map/all_gather | solution.py:123
  457.4 3.9 fusion.21
  461.4 1.1 squeeze.19
  462.5 0.3 squeeze.20
  462.9 1.2 squeeze.18
  464.0 2.5 fusion.20
  466.5 3.2 fusion.30
  469.7 1.1 copy.58
  470.8 0.3 reshape.209
  471.2 0.6 multiply_reduce_fusion.1
  471.8 0.8 multiply_convert_fusion.1
  472.6 98.1 %all-gather.11.cloned.1.call-done = bf16[256,8,1024]{2,1,0:T(8,128)(2,1)} async-done(((bf16[16,8,1024]{2,1,0:T(8,128)(2,1)}), bf16[256,8,1024]{2,1,0:T(8,128)(2,1)}) %all-gather.11.cloned.1.call-update) | async-done | bytes 4194320 | tf_op jit(solution)/shard_map/all_gather | solution.py:155
  570.7 5.6 exponential_reduce_fusion
  576.3 62.0 %all-reduce.1 = (f32[256,8]{0,1:T(8,128)S(1)}, f32[256,8]{0,1:T(8,128)S(1)}) all-reduce(f32[256,8]{0,1:T(8,128)S(1)} %get-tuple-element.6, f32[256,8]{0,1:T(8,128)S(1)} %get-tuple-element.5), channel_id=1, replica_groups=mesh['dp'=16,'tensor'=16] {'tensor'}, use_global_device_ids=true, to_apply=%region_13.14 | all-reduce | flops 4096 | bytes 32768 | tf_op jit(solution)/shard_map/psum | solution.py:162
  638.4 0.7 dynamic-slice_subtract_fusion
  (50 shorter events, 1.4 us)
Async XLA Ops:
  6.5 464.6 %copy-start = (bf16[1024,1024]{1,0:T(8,128)(2,1)S(1)}, bf16[1024,1024]{1,0:T(8,128)(2,1)}, u32[]{:S(2)}) copy-start(bf16[1024,1024]{1,0:T(8,128)(2,1)} %param.25) | copy-start | bytes 6291460
  6.5 76.7 %all-gather.5.cloned.1.call-start = ((), (), s32[]{:S(2)}) async-start(), calls=%async_computation.3 | async-start | bytes 6684672 | tf_op jit(solution)/shard_map/all_gather | solution.py:121
  8.7 127.1 %all-gather.7.cloned.1.call-start = ((), (), s32[]{:S(2)}) async-start(), calls=%async_computation.4 | async-start | bytes 2228224 | tf_op jit(solution)/shard_map/all_gather | solution.py:122
  9.4 204.5 %reduce-scatter.4.cloned.1.call-start = ((), (), s32[]{:S(2)}) async-start(), calls=%async_computation.5 | async-start | bytes 2228224 | tf_op jit(solution)/shard_map/reduce_scatter | solution.py:133
  139.5 4.2 copy-start.4
  139.5 146.3 %reduce-scatter.6.cloned.1.call-start = ((), (), s32[]{:S(2)}) async-start(), calls=%async_computation.6 | async-start | bytes 557056 | tf_op jit(solution)/shard_map/reduce_scatter | solution.py:142
  179.0 7.4 %copy-start.6 = (s32[256]{0:T(256)S(1)}, s32[256]{0:T(256)}, u32[]{:S(2)}) copy-start(s32[256]{0:T(256)} %param.28) | copy-start | bytes 3076
  185.5 28.5 %copy-start.2 = (bf16[256,1024]{1,0:T(8,128)(2,1)S(1)}, bf16[256,1024]{1,0:T(8,128)(2,1)}, u32[]{:S(2)}) copy-start(bf16[256,1024]{1,0:T(8,128)(2,1)} %param.20) | copy-start | bytes 1572868
  216.1 170.7 %reduce-scatter.8.cloned.1.call-start = ((), (), s32[]{:S(2)}) async-start(), calls=%async_computation.7 | async-start | bytes 4456448 | tf_op jit(solution)/shard_map/reduce_scatter | solution.py:93
  225.6 0.7 copy-start.8
  225.6 1.9 copy-start.3
  225.6 231.8 %copy-start.7 = (f32[1024]{0:T(1024)S(1)}, f32[1024]{0:T(1024)}, u32[]{:S(2)}) copy-start(f32[1024]{0:T(1024)} %param.23) | copy-start | bytes 12292
  225.7 231.8 %all-gather.9.cloned.1.call-start = ((), (), s32[]{:S(2)}) async-start(), calls=%async_computation.8 | async-start | bytes 6684672 | tf_op jit(solution)/shard_map/all_gather | solution.py:123
  226.3 344.5 %all-gather.11.cloned.1.call-start = ((), (), s32[]{:S(2)}) async-start(), calls=%async_computation.9 | async-start | bytes 4456448 | tf_op jit(solution)/shard_map/all_gather | solution.py:155
  466.5 4.7 copy-start.1
  466.5 5.2 copy-start.5
Sparse Core Ops, SparseCore 0:
  10.0 73.1 all-gather.4
  85.9 49.9 all-gather.6
  139.6 74.2 reduce-scatter.3
  216.3 69.4 reduce-scatter.5
  288.3 98.4 reduce-scatter.7
  389.8 67.5 all-gather.8
  472.7 97.9 all-gather.10
where the time goes:
time: 647 us; the launch traced here: 646 us
  waiting for transfers between devices  432 us (67%)
  blocking collectives  93.9 us (15%)
  local copies, waits for them, and re-layouts  54.3 us (8%)
  matrix products  29.1 us (4%)
  other arithmetic  21.4 us (3%)
  between operations  14.4 us (2%)
    reduce_scatter x1, waiting for transfers between devices, arrive_embeds(): lax.psum_scatter(embeds.astype(jnp.bfloat16), 'tensor', scatter_dimension...  100 us
    all_gather x1, waiting for transfers between devices, shards(): final_all = lax.all_gather(final, 'tensor', axis=0, tiled=True)  98.1 us
    all_gather x1, waiting for transfers between devices, shards(): lax.all_gather(qkv_weight, 'dp', axis=1, tiled=True)  70.5 us
    all_gather x1, waiting for transfers between devices, shards(): lax.all_gather(depth_qkv, 'dp', axis=1, tiled=True)  69.5 us
    psum x1, blocking collectives, shards(): exp_total, target_total = lax.psum((exp_part, target_part), 'tensor')  62 us
    all_gather x1, waiting for transfers between devices, shards(): lax.all_gather(mix_weight, 'dp', axis=1, tiled=True)  43.5 us
    gather x1, local copies, waits for them, and re-layouts, local_embeds(): code_found = code_tables[books, jnp.clip(code_local, 0, code_count - 1)]  35 us
    unnamed x1, blocking collectives  31.8 us
  transfers between devices with their start and end apart: 7, of which 7 were waited for; matrix products, arithmetic and copies ran while one was open for 12% of the time, Pallas kernels for 0%

commit v1 on v0

--- a/solution.py
+++ b/solution.py
@@ -152,7 +152,9 @@
     projected = jnp.einsum("rcd,ide->irce", dnormed, depth_full, preferred_element_type=jnp.float32)
     depth_out = depth_input + depth_mixer(projected.astype(jnp.bfloat16), depth_mix)
     final = (depth_out * rms_factor(depth_out) * final_gain).astype(jnp.bfloat16)
-    final_all = lax.all_gather(final, "tensor", axis=0, tiled=True)
+    final_all = jnp.concatenate(
+        lax.all_to_all(jnp.stack([final] * lax.axis_size("tensor")), "tensor", 0, 0), axis=0
+    )
     logits = jnp.einsum("rcd,cdv->rcv", final_all, heads_weight, preferred_element_type=jnp.float32)
     vocab_width = heads_weight.shape[2]
     target_local = codes - rank_tensor * vocab_width

time: 647 us -> 654 us (1.011)
  starting transfers between devices: 0.43 us -> 7.58 us
    all_to_all x0 -> x1, waiting for transfers between devices: none -> 98.4 us  [shards(): lax.all_to_all(jnp.stack([final] * lax.axis_size('tensor')), 'tensor', 0, 0)]
    all_gather x1 -> x0, waiting for transfers between devices: 98.1 us -> none  [shards(): final_all = lax.all_gather(final, 'tensor', axis=0, tiled=True)]
    all_to_all x0 -> x1, starting transfers between devices: none -> 7.19 us  [shards(): lax.all_to_all(jnp.stack([final] * lax.axis_size('tensor')), 'tensor', 0, 0)]
where the time goes in v1:
time: 654 us; the launch traced here: 652 us
  waiting for transfers between devices  433 us (66%)
  blocking collectives  92.2 us (14%)
  local copies, waits for them, and re-layouts  59.8 us (9%)
  matrix products  25.1 us (4%)
  other arithmetic  20.7 us (3%)
  between operations  14.4 us (2%)
  starting transfers between devices  7.58 us (1%)
    reduce_scatter x1, waiting for transfers between devices, arrive_embeds(): lax.psum_scatter(embeds.astype(jnp.bfloat16), 'tensor', scatter_dimension...  100 us
    all_to_all x1, waiting for transfers between devices, shards(): lax.all_to_all(jnp.stack([final] * lax.axis_size('tensor')), 'tensor', 0, 0)  98.4 us
    all_gather x1, waiting for transfers between devices, shards(): lax.all_gather(qkv_weight, 'dp', axis=1, tiled=True)  70.5 us
    all_gather x1, waiting for transfers between devices, shards(): lax.all_gather(depth_qkv, 'dp', axis=1, tiled=True)  69.5 us
    psum x1, blocking collectives, shards(): exp_total, target_total = lax.psum((exp_part, target_part), 'tensor')  60.3 us
    all_gather x1, waiting for transfers between devices, shards(): lax.all_gather(mix_weight, 'dp', axis=1, tiled=True)  43.5 us
    gather x1, local copies, waits for them, and re-layouts, local_embeds(): code_found = code_tables[books, jnp.clip(code_local, 0, code_count - 1)]  35 us
    unnamed x1, blocking collectives  31.8 us
  transfers between devices with their start and end apart: 7, of which 7 were waited for; matrix products, arithmetic and copies ran while one was open for 12% of the time, Pallas kernels for 0%

profile of v1, /device:TPU:8, one launch (start us, length us, event | category | flops | bytes accessed | tf_op | source)
XLA Modules:
  0.0 652.5 jit_solution(7064473601824524836)
XLA Ops:
  6.5 2.1 copy.45
  8.7 0.7 all-gather.6.cloned.1.call-update
  9.5 0.6 iota_compare_fusion.1
  10.1 2.1 multiply_reduce_fusion
  12.2 0.5 fusion.54
  12.7 70.5 %all-gather.4.cloned.1.call-done = bf16[3,4096,256]{1,2,0:T(8,128)(2,1)} async-done(((bf16[3,256,256]{1,2,0:T(8,128)(2,1)}), bf16[3,4096,256]{1,2,0:T(8,128)(2,1)}) %all-gather.4.cloned.1.call-update) | async-done | bytes 6291472 | tf_op jit(solution)/shard_map/all_gather | solution.py:121
  83.2 5.3 fusion.19
  88.6 0.6 slice.71
  90.0 1.2 fusion.24
  91.2 1.2 convolution_convert_fusion.3
  92.3 43.5 %all-gather.6.cloned.1.call-done = bf16[256,4096]{1,0:T(8,128)(2,1)} async-done(((bf16[256,256]{1,0:T(8,128)(2,1)}), bf16[256,4096]{1,0:T(8,128)(2,1)}) %all-gather.6.cloned.1.call-update) | async-done | bytes 2097168 | tf_op jit(solution)/shard_map/all_gather | solution.py:122
  135.8 3.6 convolution_convert_fusion
  139.6 4.1 convert_element_type.93
  144.0 35.0 %gather_fusion.1 = bf16[1792,1024]{1,0:T(8,128)(2,1)} fusion(bf16[7,128,1024]{2,1,0:T(8,128)(2,1)} %param.22, s32[1792]{0:T(1024)S(1)} %reshape.224), kind=kCustom, calls=%fused_computation.1 | custom fusion | bytes 7354368 | tf_op jit(solution)/shard_map/gather | solution.py:87
  179.0 6.5 reshape.231
  185.7 0.8 dynamic_slice.10
  186.5 3.4 gather_fusion
  189.9 24.1 %reduce-scatter.4.cloned.1.call-done = bf16[256,256]{1,0:T(8,128)(2,1)} async-done(((bf16[256,4096]{1,0:T(8,128)(2,1)}), bf16[256,256]{1,0:T(8,128)(2,1)}) %reduce-scatter.4.cloned.1.call-update) | async-done | bytes 131088 | tf_op jit(solution)/shard_map/reduce_scatter | solution.py:133
  214.0 2.1 convolution_convert_fusion.2
  216.1 0.2 reduce-scatter.8.cloned.1.call-start
  216.3 2.7 select_convert_fusion
  219.0 3.1 fusion.30
  222.2 3.5 pad_maximum_fusion
  225.7 0.5 all-gather.8.cloned.1.call-update
  226.3 0.6 dynamic-slice
  227.6 1.1 multiply_reduce_fusion.3
  228.7 31.8 %all-reduce = bf16[256]{0:T(256)(128)(2,1)S(1)} all-reduce(bf16[256]{0:T(256)(128)(2,1)S(1)} %multiply_reduce_fusion.3), channel_id=4, replica_groups=mesh['dp'=16,'tensor'=16] {'tensor'}, use_global_device_ids=true, to_apply=%region_5.6.clone | all-reduce | flops 256 | bytes 1024
  260.6 25.2 %reduce-scatter.6.cloned.1.call-done = bf16[16,1024]{1,0:T(8,128)(2,1)} async-done(((bf16[256,1024]{1,0:T(8,128)(2,1)}), bf16[16,1024]{1,0:T(8,128)(2,1)}) %reduce-scatter.6.cloned.1.call-update) | async-done | bytes 32784 | tf_op jit(solution)/shard_map/reduce_scatter | solution.py:142
  285.8 0.8 convert_multiply_fusion
  286.6 100.2 %reduce-scatter.8.cloned.1.call-done = bf16[16,8,1024]{2,1,0:T(8,128)(2,1)} async-done(((bf16[256,8,1024]{2,1,0:T(8,128)(2,1)}), bf16[16,8,1024]{2,1,0:T(8,128)(2,1)}) %reduce-scatter.8.cloned.1.call-update) | async-done | bytes 262160 | tf_op jit(solution)/shard_map/reduce_scatter | solution.py:93
  386.8 1.1 multiply_reduce_fusion.2
  387.9 69.5 %all-gather.8.cloned.1.call-done = bf16[3,1024,1024]{2,1,0:T(8,128)(2,1)} async-done(((bf16[3,64,1024]{2,1,0:T(8,128)(2,1)}), bf16[3,1024,1024]{2,1,0:T(8,128)(2,1)}) %all-gather.8.cloned.1.call-update) | async-done | bytes 6291472 | tf_op jit(solution)/shard_map/all_gather | solution.py:123
  457.4 3.9 fusion.16
  461.4 1.1 squeeze.19
  462.5 0.3 squeeze.20
  462.9 1.2 squeeze.18
  464.0 2.5 fusion.15
  466.5 3.2 fusion.25
  469.7 1.1 copy.58
  470.8 0.3 reshape.214
  471.2 0.6 multiply_reduce_fusion.1
  472.0 2.5 stack.2
  474.5 7.2 %all-to-all-start = ((bf16[16,16,8,1024]{3,1,2,0:T(8,128)(2,1)}), bf16[16,16,8,1024]{3,1,2,0:T(8,128)(2,1)}, u32[]{:S(2)}, u32[]{:S(2)}) async-start(bf16[16,16,8,1024]{3,1,2,0:T(8,128)(2,1)} %stack.2), calls=%async_computation.3 | async-start | bytes 8388608 | tf_op jit(solution)/shard_map/all_to_all | solution.py:156
  481.7 98.4 %all-to-all-done = bf16[16,16,8,1024]{3,1,2,0:T(8,128)(2,1)} async-done(((bf16[16,16,8,1024]{3,1,2,0:T(8,128)(2,1)}), bf16[16,16,8,1024]{3,1,2,0:T(8,128)(2,1)}, u32[]{:S(2)}, u32[]{:S(2)}) %all-to-all-start) | async-done | bytes 4194336 | tf_op jit(solution)/shard_map/all_to_all | solution.py:156
  580.1 2.8 copy.60
  583.0 1.6 exponential_reduce_fusion
  584.6 60.3 %all-reduce.1 = (f32[256,8]{0,1:T(8,128)S(1)}, f32[256,8]{0,1:T(8,128)S(1)}) all-reduce(f32[256,8]{0,1:T(8,128)S(1)} %get-tuple-element.6, f32[256,8]{0,1:T(8,128)S(1)} %get-tuple-element.5), channel_id=1, replica_groups=mesh['dp'=16,'tensor'=16] {'tensor'}, use_global_device_ids=true, to_apply=%region_13.14 | all-reduce | flops 4096 | bytes 32768 | tf_op jit(solution)/shard_map/psum | solution.py:164
  644.9 0.7 dynamic-slice_subtract_fusion
  (54 shorter events, 2.1 us)
Async XLA Ops:
  6.5 464.6 %copy-start = (bf16[1024,1024]{1,0:T(8,128)(2,1)S(1)}, bf16[1024,1024]{1,0:T(8,128)(2,1)}, u32[]{:S(2)}) copy-start(bf16[1024,1024]{1,0:T(8,128)(2,1)} %param.25) | copy-start | bytes 6291460
  6.5 76.7 %all-gather.4.cloned.1.call-start = ((), (), s32[]{:S(2)}) async-start(), calls=%async_computation.4 | async-start | bytes 6684672 | tf_op jit(solution)/shard_map/all_gather | solution.py:121
  8.7 127.1 %all-gather.6.cloned.1.call-start = ((), (), s32[]{:S(2)}) async-start(), calls=%async_computation.5 | async-start | bytes 2228224 | tf_op jit(solution)/shard_map/all_gather | solution.py:122
  9.4 204.5 %reduce-scatter.4.cloned.1.call-start = ((), (), s32[]{:S(2)}) async-start(), calls=%async_computation.6 | async-start | bytes 2228224 | tf_op jit(solution)/shard_map/reduce_scatter | solution.py:133
  139.5 4.2 copy-start.4
  139.5 146.3 %reduce-scatter.6.cloned.1.call-start = ((), (), s32[]{:S(2)}) async-start(), calls=%async_computation.7 | async-start | bytes 557056 | tf_op jit(solution)/shard_map/reduce_scatter | solution.py:142
  179.0 7.4 %copy-start.6 = (s32[256]{0:T(256)S(1)}, s32[256]{0:T(256)}, u32[]{:S(2)}) copy-start(s32[256]{0:T(256)} %param.28) | copy-start | bytes 3076
  185.5 28.5 %copy-start.2 = (bf16[256,1024]{1,0:T(8,128)(2,1)S(1)}, bf16[256,1024]{1,0:T(8,128)(2,1)}, u32[]{:S(2)}) copy-start(bf16[256,1024]{1,0:T(8,128)(2,1)} %param.20) | copy-start | bytes 1572868
  216.1 170.7 %reduce-scatter.8.cloned.1.call-start = ((), (), s32[]{:S(2)}) async-start(), calls=%async_computation.8 | async-start | bytes 4456448 | tf_op jit(solution)/shard_map/reduce_scatter | solution.py:93
  225.6 0.7 copy-start.9
  225.6 1.9 copy-start.3
  225.6 231.8 %copy-start.8 = (f32[1024]{0:T(1024)S(1)}, f32[1024]{0:T(1024)}, u32[]{:S(2)}) copy-start(f32[1024]{0:T(1024)} %param.23) | copy-start | bytes 12292
  225.7 231.8 %all-gather.8.cloned.1.call-start = ((), (), s32[]{:S(2)}) async-start(), calls=%async_computation.9 | async-start | bytes 6684672 | tf_op jit(solution)/shard_map/all_gather | solution.py:123
  466.5 4.7 copy-start.1
  466.5 5.2 copy-start.5
  474.5 105.6 %all-to-all-start = ((bf16[16,16,8,1024]{3,1,2,0:T(8,128)(2,1)}), bf16[16,16,8,1024]{3,1,2,0:T(8,128)(2,1)}, u32[]{:S(2)}, u32[]{:S(2)}) async-start(bf16[16,16,8,1024]{3,1,2,0:T(8,128)(2,1)} %stack.2), calls=%async_computation.3 | async-start | bytes 8388608 | tf_op jit(solution)/shard_map/all_to_all | solution.py:156
  580.1 2.9 copy-start.7
Sparse Core Ops, SparseCore 0:
  10.0 73.1 all-gather.3
  85.9 49.9 all-gather.5
  139.6 74.2 reduce-scatter.3
  216.3 69.4 reduce-scatter.5
  288.3 98.4 reduce-scatter.7
  389.8 67.5 all-gather.7
